TPU v7x, 256 devices: a whole 4x4x8 slice. The times are simulated.
256 devices in a mesh: dp: 8 (over y, x_hi), space: 32 (over x_lo, z, core).
Axes of the slice: x: 4 (x_hi: 2, x_lo: 2; x = x_hi * 2 + x_lo), y: 4, z: 8, core: 2. Of those that a mesh axis runs over, the one named last changes fastest.
Arguments:
- field: bfloat16 [8, 64, 1024, 1024], P('dp', None, 'space'), may hold values from -6 to 6
- cotangent: bfloat16 [8, 64, 1024, 1024], P('dp', None, 'space'), may hold values from -6 to 6
- spectral_weight: bfloat16 [64, 64, 64, 128], P('dp', 'space'), may hold values from -4 to 4
- mixing_weight: bfloat16 [64, 64], replicated, may hold values from -0.75 to 0.75
- bias: float32 [64], replicated, may hold values from -3 to 3
Outputs:
- field_grad: bfloat16 [8, 64, 1024, 1024], P('dp', None, 'space')
- spectral_grad: float32 [64, 64, 64, 128], P('dp', 'space')
- mixing_grad: float32 [64, 64], replicated
- bias_grad: float32 [64], replicated
All inputs are finite; a program needn't handle non-finite values.
Results may differ from a plain program's by a relative error of at most 0.02.
Values may be sent and summed in bfloat16 or wider, within the bound.
A program may use at most 128 MiB of HBM per device.

v0:
```python
import functools
import math

import jax
import jax.numpy as jnp
import ml_dtypes
import numpy as np
from jax import lax
from jax.experimental import pallas as pl
from jax.experimental.pallas import tpu as pltpu
from jax.sharding import PartitionSpec as P

C = 64
H = 1024
W = 1024
K1 = 64
K2 = 64
DP = 8
NZ = 8
NQ = 4
SLAB = 32
BF = jnp.bfloat16
F32 = jnp.float32
NN = (((1,), (0,)), ((), ()))
NT = (((1,), (1,)), ((), ()))


def build_tables():
    f32 = np.float32
    wpos = np.arange(W)[:, None]
    kpos = np.arange(K2)[None, :]
    angle = (wpos * kpos % W).astype(f32) * f32(2.0 * math.pi / W)
    scale = f32(1.0 / math.sqrt(W))
    cosine = np.cos(angle) * scale
    sine = np.sin(angle) * scale
    factor = np.where(kpos == 0, 1.0, 2.0).astype(f32)
    fwd = np.stack([cosine, -sine], 0).astype(ml_dtypes.bfloat16)
    inv = np.stack([factor * cosine, -factor * sine], 0).astype(ml_dtypes.bfloat16)
    z, xl, core, kk = np.meshgrid(
        np.arange(NZ), np.arange(2), np.arange(2), np.arange(2), indexing="ij"
    )
    order = (2 * (xl * 16 + z * 2 + core) + kk).reshape(-1)
    colfwd = fwd[:, :, order].transpose(1, 2, 0).reshape(W, 2 * K2)
    colinv_t = inv[:, :, order].transpose(1, 2, 0).reshape(W, 2 * K2)
    colinv = inv[:, :, order].transpose(0, 2, 1).reshape(2 * K2, W)
    colfwd_t = fwd[:, :, order].transpose(0, 2, 1).reshape(2 * K2, W)

    mpos = np.arange(K1)[:, None]
    freq = mpos + np.where(mpos >= K1 // 2, H - K1, 0)
    hpos = np.arange(H)[None, :]
    phase = (freq * hpos % H).astype(f32) * f32(2.0 * math.pi / H)
    rc = (np.cos(phase) / f32(math.sqrt(H))).astype(ml_dtypes.bfloat16)
    rs = (np.sin(phase) / f32(math.sqrt(H))).astype(ml_dtypes.bfloat16)
    fwd_rows = []
    inv_rows = []
    for zi in range(NZ):
        slabs = np.array([x * 16 + zi * 2 + c for x in range(2) for c in range(2)])
        rows = slabs[:, None, None] * SLAB + np.arange(16)[None, :, None] * 2 + np.arange(2)
        ct = rc[:, rows].reshape(DP, 8, NQ, 16, 2)
        st = rs[:, rows].reshape(DP, 8, NQ, 16, 2)
        big = np.zeros((2, 2, DP, 2, 8, NQ, 2, 2, 16), ml_dtypes.bfloat16)
        for hl in range(2):
            for k in range(2):
                big[hl, 0, :, k, :, :, k, 0] = ct[..., hl]
                big[hl, 0, :, k, :, :, k, 1] = st[..., hl]
                big[hl, 1, :, k, :, :, k, 0] = -st[..., hl]
                big[hl, 1, :, k, :, :, k, 1] = ct[..., hl]
        fwd_rows.append(big.reshape(512, 256))
        rows = slabs[:, None] * SLAB + np.arange(SLAB)[None, :]
        tab = np.zeros((2, NQ, 2, SLAB, DP, 2, 8), ml_dtypes.bfloat16)
        for i, t in enumerate((rc, rs)):
            v = t[:, rows].reshape(DP, 8, NQ, SLAB).transpose(2, 3, 0, 1)
            for k in range(2):
                tab[i, :, k, :, :, k, :] = v
        inv_rows.append(tab.reshape(512, 128))
    return colfwd, colinv_t, colinv, colfwd_t, np.stack(fwd_rows), np.stack(inv_rows)


def far_first(i):
    step = (i + 1) // 2
    return lax.rem(4 + step * (2 * lax.rem(i, 2) - 1) + 8, 8)


def kernel(
    field_h, cot_h, sw_h, colfwd_h, colinvt_h, colinv_h, colfwdt_h, rowf_h, rowi_h,
    mw, bias,
    out_h, sg_h, mg_out, bg_out,
    field, cot, pgr, mix, kron, sw, wp, colfwd, colinvt, colinv, colfwdt, rowf, rowi,
    modes, big, strip, pre, xkeep,
    qs, qr, zs, zr, ds, dr, ms, mr, gr, us, ur, sg, mg, pack, prz, pdr, pqr, pgz, pk,
    in_sem, out_sem,
    q_ss, q_rs, z_ss, z_rs, d_ss, d_rs, m_ss, m_rs, g_ss, g_rs, u_ss, u_rs,
    p_ss, p_rs,
):
    dp = lax.axis_index("dp")
    sp = lax.axis_index("space")
    z = lax.rem(sp // 2, NZ)
    q = (sp // 16) * 2 + lax.rem(sp, 2)

    def space_of(qq, zz):
        return (qq // 2) * 16 + zz * 2 + lax.rem(qq, 2)

    def quad_peer(r):
        qq = lax.rem(q + r, NQ)
        return qq, {"space": space_of(qq, z)}

    def z_peer(off):
        zz = lax.rem(z + off, NZ)
        return zz, {"space": space_of(q, zz)}

    def dp_peer(r):
        dd = lax.rem(dp + r, DP)
        return dd, {"dp": dd}

    def remote(src, dst, ss, rs, dev):
        return pltpu.make_async_remote_copy(
            src_ref=src, dst_ref=dst, send_sem=ss, recv_sem=rs,
            device_id=dev, device_id_type=pl.DeviceIdType.MESH,
        )

    loads = [
        pltpu.make_async_copy(colfwd_h, colfwd, in_sem.at[0]),
        *[
            pltpu.make_async_copy(
                field_h.at[0, pl.ds(16 * i, 16)], field.at[pl.ds(16 * i, 16)], in_sem.at[1 + i]
            )
            for i in range(4)
        ],
        pltpu.make_async_copy(rowf_h.at[z], rowf, in_sem.at[5]),
        pltpu.make_async_copy(sw_h, sw, in_sem.at[6]),
        pltpu.make_async_copy(rowi_h.at[z], rowi, in_sem.at[7]),
        pltpu.make_async_copy(colinv_h, colinv, in_sem.at[8]),
        pltpu.make_async_copy(cot_h.at[0], cot, in_sem.at[9]),
        pltpu.make_async_copy(colinvt_h, colinvt, in_sem.at[10]),
        pltpu.make_async_copy(colfwdt_h, colfwdt, in_sem.at[11]),
    ]
    for copy in loads:
        copy.start()

    barrier = pltpu.get_barrier_semaphore()
    for r in range(1, NQ):
        pl.semaphore_signal(barrier, 1, device_id=quad_peer(r)[1], device_id_type=pl.DeviceIdType.MESH)
    for r in range(1, NZ):
        pl.semaphore_signal(barrier, 1, device_id=z_peer(r)[1], device_id_type=pl.DeviceIdType.MESH)
    for r in range(1, DP):
        pl.semaphore_signal(barrier, 1, device_id=dp_peer(r)[1], device_id_type=pl.DeviceIdType.MESH)

    low = lax.broadcasted_iota(jnp.int32, (64, 128), 1) < 64
    sign = jnp.where(low, -1.0, 1.0).astype(F32)
    low128 = lax.broadcasted_iota(jnp.int32, (128, 128), 1) < 64
    sign256 = jnp.where(lax.broadcasted_iota(jnp.int32, (256, 128), 1) < 64, -1.0, 1.0).astype(F32)

    loads[0].wait()
    for i in range(4):
        loads[1 + i].wait()
        for j in range(2):
            rows = field[16 * i + 8 * j : 16 * i + 8 * j + 8].reshape(256, W)
            modes[512 * i + 256 * j : 512 * i + 256 * j + 256, :] = lax.dot_general(
                rows, colfwd[...], NN, preferred_element_type=F32
            )
    pl.semaphore_wait(barrier, NQ + NZ + DP - 3)

    def build_kron(transposed):
        spread = (
            lax.broadcasted_iota(jnp.int32, (1024, 64), 0) // 16
            == lax.broadcasted_iota(jnp.int32, (1024, 64), 1)
        ).astype(F32).astype(BF)
        half = lax.dot_general(
            spread, mw[...], NT if transposed else NN, preferred_element_type=F32
        ).astype(BF)
        same = lax.rem(lax.broadcasted_iota(jnp.int32, (256, 1024), 0), 16) == lax.rem(
            lax.broadcasted_iota(jnp.int32, (256, 1024), 1), 16
        )
        for i in range(4):
            full = lax.dot_general(
                half[256 * i : 256 * i + 256], spread, NT, preferred_element_type=F32
            )
            kron[256 * i : 256 * i + 256, :] = jnp.where(same, full, 0.0).astype(BF)

    def pointwise_tile(source, i):
        hb = pl.multiple_of((i // 4) * 16, 16)
        wq = pl.multiple_of(lax.rem(i, 4) * 256, 256)
        rhs = source[:, pl.ds(hb, 16), pl.ds(wq, 256)].reshape(1024, 256)
        res = lax.dot_general(kron[...], rhs, NN, preferred_element_type=F32)
        mix[:, pl.ds(hb, 16), pl.ds(wq, 256)] = res.reshape(64, 16, 256)

    def mixgrad_tile(i):
        hb = pl.multiple_of((i // 4) * 16, 16)
        cb = pl.multiple_of(lax.rem(i, 4) * 16, 16)
        lhs = field[pl.ds(cb, 16), pl.ds(hb, 16), :].reshape(256, W)
        rhs = pgr[:, pl.ds(hb, 16), :].reshape(1024, W)
        res = lax.dot_general(lhs, rhs, NT, preferred_element_type=F32)
        same = lax.rem(lax.broadcasted_iota(jnp.int32, (256, 1024), 0), 16) == lax.rem(
            lax.broadcasted_iota(jnp.int32, (256, 1024), 1), 16
        )
        res = jnp.where(same, res, 0.0).reshape(16, 16, 1024).sum(1)
        mg[pl.ds(cb, 16), :] = mg[pl.ds(cb, 16), :] + res

    def quad_send(ph):
        def turn(h2, total):
            a = modes[pl.ds(2 * h2, 64, stride=SLAB), :]
            b = modes[pl.ds(2 * h2 + 1, 64, stride=SLAB), :]
            big[pl.ds(pl.multiple_of(h2 * 128, 128), 128), :] = jnp.concatenate([a, b], 0).T
            return total + a + b

        total = lax.fori_loop(0, 16, turn, jnp.zeros((64, 128), F32))

        def chunk(i, carry):
            zc = lax.rem(z + far_first(i), NZ)
            for qq in range(NQ):
                for kr in range(4):
                    v = big[pl.ds((zc * NQ + qq) * 4 + kr, 16, stride=128), :]
                    qs[ph, zc, qq, kr * 16 : kr * 16 + 16, :] = v.astype(BF)
            for r in range(1, NQ):
                qq, dev = quad_peer(r)
                remote(
                    qs.at[ph, zc, qq], qr.at[ph, zc, q], q_ss.at[ph, zc, qq], q_rs.at[ph, zc, q], dev
                ).start()
            qr[ph, zc, q] = qs[ph, zc, q]
            return carry

        lax.fori_loop(0, NZ, chunk, 0)
        return total

    def quad_to_z(ph, idle):
        def chunk(i, carry):
            zc = lax.rem(z + far_first(i), NZ)
            for r in range(1, NQ):
                qq, dev = quad_peer(r)
                remote(
                    qs.at[ph, zc, qq], qr.at[ph, zc, qq], q_ss.at[ph, zc, qq], q_rs.at[ph, zc, qq], dev
                ).wait_recv()
            x = qr[ph, zc].reshape(256, 128)
            b = lax.dot_general(rowf[...], x, NN, preferred_element_type=F32)
            straight = jnp.where(low128, b[0:128], b[384:512])
            crossed = jnp.where(low128, b[128:256], b[256:384])
            zs[ph, zc] = (straight + pltpu.roll(crossed, 64, 1)).astype(BF)

            @pl.when(i < 7)
            def _():
                remote(
                    zs.at[ph, zc], zr.at[ph, z], z_ss.at[ph, zc], z_rs.at[ph, z],
                    {"space": space_of(q, zc)},
                ).start()

            idle(i)
            return carry

        lax.fori_loop(0, NZ, chunk, 0)
        total = zs[ph, z].astype(F32)
        for r in range(1, NZ):
            zz, dev = z_peer(r)
            remote(zs.at[ph, zz], zr.at[ph, zz], z_ss.at[ph, zz], z_rs.at[ph, zz], dev).wait_recv()
            total = total + zr[ph, zz].astype(F32)
        return total.astype(BF)

    def dp_out(ph, src, dst, ss, rs, value):
        src[ph] = value.reshape(DP, 16, 128)
        for r in range(1, DP):
            dd, dev = dp_peer(r)
            remote(src.at[ph, dd], dst.at[ph, dp], ss.at[ph, dd], rs.at[ph, dp], dev).start()
        dst[ph, dp] = src[ph, dp]

    def dp_in(ph, src, dst, ss, rs):
        for r in range(1, DP):
            dd, dev = dp_peer(r)
            remote(src.at[ph, dd], dst.at[ph, dd], ss.at[ph, dd], rs.at[ph, dd], dev).wait_recv()
        return dst[ph].reshape(128, 128)

    row_mk = lax.rem(lax.broadcasted_iota(jnp.int32, (128, 128), 0), 16)
    col_mk = lax.rem(lax.broadcasted_iota(jnp.int32, (128, 128), 1), 16)

    def per_mode(x, dims):
        total = jnp.zeros((128, 128), F32)
        for mk in range(16):
            mine = jnp.where(row_mk == mk, x.astype(F32), 0.0).astype(BF)
            total = total + lax.dot_general(mine, wp[mk], dims, preferred_element_type=F32)
        return total.astype(BF)

    def z_send(ph):
        def one(i, carry):
            zz = lax.rem(z + far_first(i), NZ)
            remote(
                mr.at[ph], gr.at[ph, z], g_ss.at[ph, zz], g_rs.at[ph, z], {"space": space_of(q, zz)}
            ).start()
            return carry

        lax.fori_loop(0, 7, one, 0)
        gr[ph, z] = mr[ph]

    def z_to_quad(ph, idle):
        def source(j, carry):
            zc = lax.rem(z + far_first(7 - j), NZ)

            @pl.when(j > 0)
            def _():
                remote(
                    mr.at[ph], gr.at[ph, zc], g_ss.at[ph, zc], g_rs.at[ph, zc],
                    {"space": space_of(q, lax.rem(z + jnp.maximum(far_first(7 - j), 1), NZ))},
                ).wait_recv()

            t = lax.dot_general(
                rowi[...], gr[ph, zc].reshape(128, 128), NN, preferred_element_type=F32
            )
            v = t[0:256] + pltpu.roll(t[256:512], 64, 1) * sign256
            us[ph, zc] = v.astype(BF).reshape(NQ, 64, 128)
            for r in range(1, NQ):
                qq, dev = quad_peer(r)
                remote(
                    us.at[ph, zc, qq], ur.at[ph, zc, q], u_ss.at[ph, zc, qq], u_rs.at[ph, zc, q], dev
                ).start()
            ur[ph, zc, q] = us[ph, zc, q]
            idle(j)
            return carry

        lax.fori_loop(0, NZ, source, 0)

        def take(j, carry):
            zc = lax.rem(z + far_first(7 - j), NZ)
            for r in range(1, NQ):
                qq, dev = quad_peer(r)
                remote(
                    us.at[ph, zc, qq], ur.at[ph, zc, qq], u_ss.at[ph, zc, qq], u_rs.at[ph, zc, qq], dev
                ).wait_recv()
            for qq in range(NQ):
                for k in range(2):
                    v = ur[ph, zc, qq, k * 32 : k * 32 + 32, :].astype(F32)
                    big[pl.ds((zc * NQ + qq) * 2 + k, SLAB, stride=64), :] = v
            return carry

        lax.fori_loop(0, NZ, take, 0)

        def turn(h2, carry):
            t = big[pl.ds(pl.multiple_of(h2 * 128, 128), 128), :].T
            re, im = t[0:64], t[64:128]
            modes[pl.ds(2 * h2, 64, stride=SLAB), :] = jnp.where(low, re, pltpu.roll(im, 64, 1))
            modes[pl.ds(2 * h2 + 1, 64, stride=SLAB), :] = jnp.where(low, pltpu.roll(re, 64, 1), im)
            return carry

        lax.fori_loop(0, 16, turn, 0)

    def nothing(i):
        pass

    quad_send(0)
    build_kron(True)
    loads[5].wait()
    x = quad_to_z(0, functools.partial(pointwise_tile, field))
    dp_out(0, ds, dr, d_ss, d_rs, x)
    loads[6].wait()
    for m in range(8):
        for k in range(2):
            top = sw[m, k].astype(F32)
            bottom = pltpu.roll(top, 64, 1) * sign
            wp[k * 8 + m] = jnp.concatenate([top, bottom], 0).astype(BF)
    mode_rows = dp_in(0, ds, dr, d_ss, d_rs)
    xkeep[...] = mode_rows
    dp_out(0, ms, mr, m_ss, m_rs, per_mode(mode_rows, NN))
    mg[...] = jnp.zeros_like(mg)
    dp_in(0, ms, mr, m_ss, m_rs)
    z_send(0)
    loads[7].wait()
    z_to_quad(0, nothing)

    loads[8].wait()
    loads[9].wait()
    loads[10].wait()
    c1 = math.sqrt(2.0 / math.pi)
    c3 = c1 * 0.044715

    def section(blk, carry):
        r0 = pl.multiple_of(blk * 256, 256)
        pre[...] = lax.dot_general(
            modes[pl.ds(r0, 256), :].astype(BF), colinv[...], NN, preferred_element_type=F32
        )

        def tile(t, inner):
            ch = blk * 8 + t // 2
            hh = pl.multiple_of(lax.rem(t, 2) * 16, 16)
            v = (
                pre[pl.ds(pl.multiple_of(t * 16, 16), 16), :]
                + mix[ch, pl.ds(hh, 16), :]
                + bias[ch]
            )
            v2 = v * v
            th = jnp.tanh(v * (c1 + c3 * v2))
            slope = (0.5 + 0.5 * th) + (v * (0.5 * c1 + 1.5 * c3 * v2)) * (1.0 - th * th)
            pgr[ch, pl.ds(hh, 16), :] = (cot[ch, pl.ds(hh, 16), :].astype(F32) * slope).astype(BF)
            return inner

        lax.fori_loop(0, 16, tile, 0)
        grads = pgr[pl.ds(pl.multiple_of(blk * 8, 8), 8)].reshape(256, W)
        modes[pl.ds(r0, 256), :] = lax.dot_general(
            grads, colinvt[...], NN, preferred_element_type=F32
        )
        return carry

    lax.fori_loop(0, 8, section, 0)

    total = quad_send(1)
    strip[...] = total.T
    build_kron(False)
    g = quad_to_z(1, mixgrad_tile)
    dp_out(1, ds, dr, d_ss, d_rs, g)

    spread = (
        lax.broadcasted_iota(jnp.int32, (1024, 64), 0) // 16
        == lax.broadcasted_iota(jnp.int32, (1024, 64), 1)
    ).astype(F32).astype(BF)
    part = mg[...]
    hi = part.astype(BF)
    rest = part - hi.astype(F32)
    mid = rest.astype(BF)
    lo = (rest - mid.astype(F32)).astype(BF)
    part = (
        lax.dot_general(hi, spread, NN, preferred_element_type=F32)
        + lax.dot_general(mid, spread, NN, preferred_element_type=F32)
        + lax.dot_general(lo, spread, NN, preferred_element_type=F32)
    )
    bias_row = jnp.concatenate([strip[0:1, :] * 32.0, jnp.zeros((63, 64), F32)], 0)
    pack[...] = jnp.concatenate([part, bias_row], 1).reshape(NZ, 8, 128)
    for r in range(1, NZ):
        zz, dev = z_peer(r)
        remote(pack.at[zz], prz.at[z], p_ss.at[0, zz], p_rs.at[0, z], dev).start()
    prz[z] = pack[z]

    grad_rows = dp_in(1, ds, dr, d_ss, d_rs)
    dp_out(1, ms, mr, m_ss, m_rs, per_mode(grad_rows, NT))

    for r in range(1, NZ):
        zz, dev = z_peer(r)
        remote(pack.at[zz], prz.at[zz], p_ss.at[0, zz], p_rs.at[0, zz], dev).wait_recv()
    pk[0] = prz[...].sum(0)
    for r in range(1, DP):
        dd, dev = dp_peer(r)
        remote(pk.at[0], pdr.at[dp], p_ss.at[1, dd], p_rs.at[1, dp], dev).start()
    pdr[dp] = pk[0]

    x_t = xkeep[...].astype(F32).T
    for m in range(8):
        for k in range(2):
            mine = jnp.where(col_mk == k * 8 + m, x_t, 0.0).astype(BF)
            prod = lax.dot_general(mine, grad_rows, NN, preferred_element_type=F32)
            sg[m, k] = prod[0:64] - pltpu.roll(prod[64:128], 64, 1) * sign
    sg_copy = pltpu.make_async_copy(sg, sg_h, out_sem.at[8])
    sg_copy.start()

    dp_in(1, ms, mr, m_ss, m_rs)
    z_send(1)

    for r in range(1, DP):
        dd, dev = dp_peer(r)
        remote(pk.at[0], pdr.at[dd], p_ss.at[1, dd], p_rs.at[1, dd], dev).wait_recv()
    pk[1] = pdr[...].sum(0)
    for r in range(1, NQ):
        qq, dev = quad_peer(r)
        remote(pk.at[1], pqr.at[q], p_ss.at[2, qq], p_rs.at[2, q], dev).start()
    pqr[q] = pk[1]

    z_to_quad(1, functools.partial(pointwise_tile, pgr))

    for r in range(1, NQ):
        qq, dev = quad_peer(r)
        remote(pk.at[1], pqr.at[qq], p_ss.at[2, qq], p_rs.at[2, qq], dev).wait_recv()
    pk[2] = pqr[...].sum(0)
    for r in range(1, NZ):
        zz, dev = z_peer(r)
        remote(pk.at[2], pgz.at[z], p_ss.at[3, zz], p_rs.at[3, z], dev).start()
    pgz[z] = pk[2]

    loads[11].wait()
    for blk in range(8):
        rows = lax.dot_general(
            modes[256 * blk : 256 * blk + 256, :].astype(BF), colfwdt[...], NN,
            preferred_element_type=F32,
        )
        chs = slice(8 * blk, 8 * blk + 8)
        cot[chs] = (rows.reshape(8, SLAB, W) + mix[chs]).astype(BF)
        pltpu.make_async_copy(cot.at[chs], out_h.at[0, chs], out_sem.at[blk]).start()

    for r in range(1, NZ):
        zz, dev = z_peer(r)
        remote(pk.at[2], pgz.at[zz], p_ss.at[3, zz], p_rs.at[3, zz], dev).wait_recv()
    norm = 1.0 / math.sqrt(DP * H * W)
    whole = pgz[...].reshape(64, 128) * norm
    mg_out[...] = whole[:, 0:64]
    bg_out[...] = whole[0:1, 64:128]

    for ph in range(2):

        def drain(i, carry):
            for r in range(1, NQ):
                qq, dev = quad_peer(r)
                remote(
                    qs.at[ph, i, qq], qr.at[ph, i, q], q_ss.at[ph, i, qq], q_rs.at[ph, i, q], dev
                ).wait_send()
                remote(
                    us.at[ph, i, qq], ur.at[ph, i, q], u_ss.at[ph, i, qq], u_rs.at[ph, i, q], dev
                ).wait_send()
            return carry

        lax.fori_loop(0, NZ, drain, 0)
        for r in range(1, NZ):
            zz, dev = z_peer(r)
            remote(zs.at[ph, zz], zr.at[ph, z], z_ss.at[ph, zz], z_rs.at[ph, z], dev).wait_send()
            remote(mr.at[ph], gr.at[ph, z], g_ss.at[ph, zz], g_rs.at[ph, z], dev).wait_send()
            dd, dev = dp_peer(r)
            remote(ds.at[ph, dd], dr.at[ph, dp], d_ss.at[ph, dd], d_rs.at[ph, dp], dev).wait_send()
            remote(ms.at[ph, dd], mr.at[ph, dp], m_ss.at[ph, dd], m_rs.at[ph, dp], dev).wait_send()
    for r in range(1, NZ):
        zz, dev = z_peer(r)
        remote(pack.at[zz], prz.at[z], p_ss.at[0, zz], p_rs.at[0, z], dev).wait_send()
        remote(pk.at[2], pgz.at[z], p_ss.at[3, zz], p_rs.at[3, z], dev).wait_send()
        dd, dev = dp_peer(r)
        remote(pk.at[0], pdr.at[dp], p_ss.at[1, dd], p_rs.at[1, dp], dev).wait_send()
    for r in range(1, NQ):
        qq, dev = quad_peer(r)
        remote(pk.at[1], pqr.at[q], p_ss.at[2, qq], p_rs.at[2, q], dev).wait_send()
    for blk in range(8):
        chs = slice(8 * blk, 8 * blk + 8)
        pltpu.make_async_copy(cot.at[chs], out_h.at[0, chs], out_sem.at[blk]).wait()
    sg_copy.wait()


def per_device(field, cotangent, spectral_weight, mixing_weight, bias):
    tables = [jnp.asarray(t) for t in build_tables()]
    hbm = pl.BlockSpec(memory_space=pl.ANY)
    vmem = pl.BlockSpec(memory_space=pltpu.VMEM)
    smem = pl.BlockSpec(memory_space=pltpu.SMEM)
    dma = pltpu.SemaphoreType.DMA
    out = pl.pallas_call(
        kernel,
        out_shape=(
            jax.ShapeDtypeStruct((1, C, SLAB, W), BF),
            jax.ShapeDtypeStruct((8, 2, C, 2 * C), F32),
            jax.ShapeDtypeStruct((C, C), F32),
            jax.ShapeDtypeStruct((1, C), F32),
        ),
        in_specs=[hbm] * 9 + [vmem, smem],
        out_specs=(hbm, hbm, vmem, vmem),
        scratch_shapes=[
            pltpu.VMEM((C, SLAB, W), BF),
            pltpu.VMEM((C, SLAB, W), BF),
            pltpu.VMEM((C, SLAB, W), BF),
            pltpu.VMEM((C, SLAB, W), F32),
            pltpu.VMEM((1024, 1024), BF),
            pltpu.VMEM((8, 2, C, 2 * C), BF),
            pltpu.VMEM((16, 128, 128), BF),
            pltpu.VMEM((W, 128), BF),
            pltpu.VMEM((W, 128), BF),
            pltpu.VMEM((128, W), BF),
            pltpu.VMEM((128, W), BF),
            pltpu.VMEM((512, 256), BF),
            pltpu.VMEM((512, 128), BF),
            pltpu.VMEM((C * SLAB, 128), F32),
            pltpu.VMEM((C * SLAB, 128), F32),
            pltpu.VMEM((128, C), F32),
            pltpu.VMEM((256, W), F32),
            pltpu.VMEM((128, 128), BF),
            pltpu.VMEM((2, NZ, NQ, 64, 128), BF),
            pltpu.VMEM((2, NZ, NQ, 64, 128), BF),
            pltpu.VMEM((2, NZ, 128, 128), BF),
            pltpu.VMEM((2, NZ, 128, 128), BF),
            pltpu.VMEM((2, DP, 16, 128), BF),
            pltpu.VMEM((2, DP, 16, 128), BF),
            pltpu.VMEM((2, DP, 16, 128), BF),
            pltpu.VMEM((2, DP, 16, 128), BF),
            pltpu.VMEM((2, NZ, DP, 16, 128), BF),
            pltpu.VMEM((2, NZ, NQ, 64, 128), BF),
            pltpu.VMEM((2, NZ, NQ, 64, 128), BF),
            pltpu.VMEM((8, 2, C, 2 * C), F32),
            pltpu.VMEM((C, 1024), F32),
            pltpu.VMEM((NZ, 8, 128), F32),
            pltpu.VMEM((NZ, 8, 128), F32),
            pltpu.VMEM((DP, 8, 128), F32),
            pltpu.VMEM((NQ, 8, 128), F32),
            pltpu.VMEM((NZ, 8, 128), F32),
            pltpu.VMEM((3, 8, 128), F32),
            dma((12,)),
            dma((9,)),
            dma((2, NZ, NQ)), dma((2, NZ, NQ)),
            dma((2, NZ)), dma((2, NZ)),
            dma((2, DP)), dma((2, DP)),
            dma((2, DP)), dma((2, DP)),
            dma((2, NZ)), dma((2, NZ)),
            dma((2, NZ, NQ)), dma((2, NZ, NQ)),
            dma((4, 8)), dma((4, 8)),
        ],
        compiler_params=pltpu.CompilerParams(
            collective_id=0, has_side_effects=True, vmem_limit_bytes=58 * 1024 * 1024
        ),
        cost_estimate=pl.CostEstimate(
            flops=20_000_000_000, bytes_accessed=16_000_000, transcendentals=2_000_000
        ),
    )(field, cotangent, spectral_weight, *tables, mixing_weight, bias)
    field_grad, spectral_grad, mixing_grad, bias_grad = out
    return field_grad, spectral_grad, mixing_grad, bias_grad.reshape(C)


def solution(mesh):
    return jax.shard_map(
        per_device,
        mesh=mesh,
        in_specs=(
            P("dp", None, "space", None),
            P("dp", None, "space", None),
            P("dp", "space", None, None),
            P(),
            P(),
        ),
        out_specs=(P("dp", None, "space", None), P("dp", "space", None, None), P(), P()),
        check_vma=False,
    )
```

profile of v0, /device:TPU:1, one launch (start us, length us, event | category | flops | bytes accessed | tf_op | source)
XLA Modules:
  0.0 123.2 jit_solution(6314528939834427215)
XLA Ops:
  0.6 115.6 %shard_map.138 = (bf16[1,64,32,1024]{3,2,1,0:T(8,128)(2,1)}, f32[8,2,64,128]{3,2,1,0:T(8,128)}, f32[64,64]{1,0:T(8,128)}, f32[1,64]{1,0:T(1,128)}) custom-call(bf16[1,64,32,1024]{3,2,1,0:T(8,128)(2,1)} %field_h.1, bf16[1,64,32,1024]{3,2,1,0:T(8,128)(2,1)} %cot_h.1, bf16[8,2,64,128]{3,2,1,0:T(8,128)(2,1)} %sw_h.1, bf16[1024,128]{1,0:T(8,128)(2,1)} %constant.12.clone.colfwd_h, ...), custom_call_target="tpu_custom_call" | custom-call | flops 20000000000 | bytes 16000000 | tf_op jit(solution)/shard_map/pallas_call | solution.py:531
  116.2 0.0 copy-start
  116.2 0.0 copy-start.1
  116.2 0.0 copy-start.2
  116.2 5.1 %copy.19 = bf16[1,64,32,1024]{3,2,1,0:T(8,128)(2,1)} copy(bf16[1,64,32,1024]{3,2,1,0:T(8,128)(2,1)} %get-tuple-element.16) | data formatting | bytes 8388608
  121.3 0.0 copy-done
  121.3 0.8 copy.20
  122.1 0.0 copy-done.1
  122.1 0.6 copy.21
  122.7 0.0 copy-done.2
  122.7 0.5 copy.22
Async XLA Ops:
  116.2 5.1 %copy-start = (f32[8,2,64,128]{3,2,1,0:T(8,128)S(1)}, f32[8,2,64,128]{3,2,1,0:T(8,128)}, u32[]{:S(2)}) copy-start(f32[8,2,64,128]{3,2,1,0:T(8,128)} %get-tuple-element.17) | copy-start | bytes 1572868
  116.2 5.9 %copy-start.1 = (f32[64,64]{1,0:T(8,128)S(1)}, f32[64,64]{1,0:T(8,128)}, u32[]{:S(2)}) copy-start(f32[64,64]{1,0:T(8,128)} %get-tuple-element.18) | copy-start | bytes 49156
  116.2 6.5 %copy-start.2 = (f32[1,64]{1,0:T(1,128)S(1)}, f32[1,64]{1,0:T(1,128)}, u32[]{:S(2)}) copy-start(f32[1,64]{1,0:T(1,128)} %get-tuple-element.11) | copy-start | bytes 772
where the time goes:
time: 123 us
  Pallas kernels  116 us (94%)
  local copies, waits for them, and re-layouts  7 us (6%)
    pallas_call x1, Pallas kernels, per_device(): pl.pallas_call(kernel, out_shape=(jax.ShapeDtypeStruct((1, C, SLAB, W), B...  116 us
    unnamed x10, local copies, waits for them, and re-layouts  7 us

commit v1 on v0

--- a/solution.py
+++ b/solution.py
@@ -73,7 +73,14 @@
             for k in range(2):
                 tab[i, :, k, :, :, k, :] = v
         inv_rows.append(tab.reshape(512, 128))
-    return colfwd, colinv_t, colinv, colfwd_t, np.stack(fwd_rows), np.stack(inv_rows)
+    i = np.arange(256)
+    sources = (
+        32 * (i % 8) + i // 8,
+        8 * (i % 32) + i // 32,
+        16 * (i % 16) + i // 16,
+    )
+    perms = np.stack([np.eye(256)[s] for s in sources]).astype(ml_dtypes.bfloat16)
+    return colfwd, colinv_t, colinv, colfwd_t, np.stack(fwd_rows), np.stack(inv_rows), perms
 
 
 def far_first(i):
@@ -82,11 +89,11 @@
 
 
 def kernel(
-    field_h, cot_h, sw_h, colfwd_h, colinvt_h, colinv_h, colfwdt_h, rowf_h, rowi_h,
+    field_h, cot_h, sw_h, colfwd_h, colinvt_h, colinv_h, rowf_h, rowi_h, perm_h,
     mw, bias,
-    out_h, sg_h, mg_out, bg_out,
-    field, cot, pgr, mix, kron, sw, wp, colfwd, colinvt, colinv, colfwdt, rowf, rowi,
-    modes, big, strip, pre, xkeep,
+    pm_h, l_h, sg_h, mg_out, bg_out,
+    field, cot, pgr, mix, kron, sw, wp, colfwd, colinvt, colinv, rowf, rowi,
+    perm, slab, big, back, lrows, pre0, pre1, xkeep, strip,
     qs, qr, zs, zr, ds, dr, ms, mr, gr, us, ur, sg, mg, pack, prz, pdr, pqr, pgz, pk,
     in_sem, out_sem,
     q_ss, q_rs, z_ss, z_rs, d_ss, d_rs, m_ss, m_rs, g_ss, g_rs, u_ss, u_rs,
@@ -122,19 +129,19 @@
         pltpu.make_async_copy(colfwd_h, colfwd, in_sem.at[0]),
         *[
             pltpu.make_async_copy(
-                field_h.at[0, pl.ds(16 * i, 16)], field.at[pl.ds(16 * i, 16)], in_sem.at[1 + i]
+                field_h.at[0, pl.ds(8 * i, 8)], field.at[pl.ds(8 * i, 8)], in_sem.at[1 + i]
             )
-            for i in range(4)
+            for i in range(8)
         ],
-        pltpu.make_async_copy(rowf_h.at[z], rowf, in_sem.at[5]),
-        pltpu.make_async_copy(sw_h, sw, in_sem.at[6]),
-        pltpu.make_async_copy(rowi_h.at[z], rowi, in_sem.at[7]),
-        pltpu.make_async_copy(colinv_h, colinv, in_sem.at[8]),
-        pltpu.make_async_copy(cot_h.at[0], cot, in_sem.at[9]),
-        pltpu.make_async_copy(colinvt_h, colinvt, in_sem.at[10]),
-        pltpu.make_async_copy(colfwdt_h, colfwdt, in_sem.at[11]),
+        pltpu.make_async_copy(perm_h, perm, in_sem.at[15]),
+        pltpu.make_async_copy(rowf_h.at[z], rowf, in_sem.at[9]),
+        pltpu.make_async_copy(sw_h, sw, in_sem.at[10]),
+        pltpu.make_async_copy(rowi_h.at[z], rowi, in_sem.at[11]),
+        pltpu.make_async_copy(colinv_h, colinv, in_sem.at[12]),
+        pltpu.make_async_copy(colinvt_h, colinvt, in_sem.at[13]),
+        pltpu.make_async_copy(cot_h.at[0], cot, in_sem.at[14]),
     ]
-    for copy in loads:
+    for copy in loads[:11]:
         copy.start()
 
     barrier = pltpu.get_barrier_semaphore()
@@ -150,17 +157,28 @@
     low128 = lax.broadcasted_iota(jnp.int32, (128, 128), 1) < 64
     sign256 = jnp.where(lax.broadcasted_iota(jnp.int32, (256, 128), 1) < 64, -1.0, 1.0).astype(F32)
 
+    def to_slab(blk, rows):
+        res = lax.dot_general(perm[0], rows.astype(BF), NN, preferred_element_type=F32)
+        slab[:, pl.ds(blk * 8 if isinstance(blk, int) else pl.multiple_of(blk * 8, 8), 8), :] = (
+            res.reshape(SLAB, 8, 128)
+        )
+
+    def from_slab(blk):
+        start = blk * 8 if isinstance(blk, int) else pl.multiple_of(blk * 8, 8)
+        rows = slab[:, pl.ds(start, 8), :].reshape(256, 128).astype(BF)
+        return lax.dot_general(perm[1], rows, NN, preferred_element_type=F32).astype(BF)
+
     loads[0].wait()
-    for i in range(4):
+    loads[9].wait()
+    for i in range(8):
         loads[1 + i].wait()
-        for j in range(2):
-            rows = field[16 * i + 8 * j : 16 * i + 8 * j + 8].reshape(256, W)
-            modes[512 * i + 256 * j : 512 * i + 256 * j + 256, :] = lax.dot_general(
-                rows, colfwd[...], NN, preferred_element_type=F32
-            )
+        rows = field[8 * i : 8 * i + 8].reshape(256, W)
+        to_slab(i, lax.dot_general(rows, colfwd[...], NN, preferred_element_type=F32))
+    for copy in loads[11:]:
+        copy.start()
     pl.semaphore_wait(barrier, NQ + NZ + DP - 3)
 
-    def build_kron(transposed):
+    def build_kron(n, transposed):
         spread = (
             lax.broadcasted_iota(jnp.int32, (1024, 64), 0) // 16
             == lax.broadcasted_iota(jnp.int32, (1024, 64), 1)
@@ -175,14 +193,21 @@
             full = lax.dot_general(
                 half[256 * i : 256 * i + 256], spread, NT, preferred_element_type=F32
             )
-            kron[256 * i : 256 * i + 256, :] = jnp.where(same, full, 0.0).astype(BF)
-
-    def pointwise_tile(source, i):
+            kron[n, 256 * i : 256 * i + 256, :] = jnp.where(same, full, 0.0).astype(BF)
+
+    def pointwise_tile(n, source, target, i):
         hb = pl.multiple_of((i // 4) * 16, 16)
         wq = pl.multiple_of(lax.rem(i, 4) * 256, 256)
         rhs = source[:, pl.ds(hb, 16), pl.ds(wq, 256)].reshape(1024, 256)
-        res = lax.dot_general(kron[...], rhs, NN, preferred_element_type=F32)
-        mix[:, pl.ds(hb, 16), pl.ds(wq, 256)] = res.reshape(64, 16, 256)
+        res = lax.dot_general(kron[n], rhs, NN, preferred_element_type=F32)
+        target[:, pl.ds(hb, 16), pl.ds(wq, 256)] = res.reshape(64, 16, 256).astype(target.dtype)
+
+    def some(tile, first, last):
+        def one(i, carry):
+            tile(i)
+            return carry
+
+        lax.fori_loop(first, last, one, 0)
 
     def mixgrad_tile(i):
         hb = pl.multiple_of((i // 4) * 16, 16)
@@ -197,20 +222,15 @@
         mg[pl.ds(cb, 16), :] = mg[pl.ds(cb, 16), :] + res
 
     def quad_send(ph):
-        def turn(h2, total):
-            a = modes[pl.ds(2 * h2, 64, stride=SLAB), :]
-            b = modes[pl.ds(2 * h2 + 1, 64, stride=SLAB), :]
-            big[pl.ds(pl.multiple_of(h2 * 128, 128), 128), :] = jnp.concatenate([a, b], 0).T
-            return total + a + b
-
-        total = lax.fori_loop(0, 16, turn, jnp.zeros((64, 128), F32))
+        for h2 in range(16):
+            big[h2] = slab[2 * h2 : 2 * h2 + 2].reshape(128, 128).T.astype(BF)
+        for zc in range(NZ):
+            rows = big[:, zc * 16 : zc * 16 + 16, :].reshape(256, 128)
+            res = lax.dot_general(perm[2], rows, NN, preferred_element_type=F32)
+            qs[ph, zc] = res.astype(BF).reshape(NQ, 64, 128)
 
         def chunk(i, carry):
             zc = lax.rem(z + far_first(i), NZ)
-            for qq in range(NQ):
-                for kr in range(4):
-                    v = big[pl.ds((zc * NQ + qq) * 4 + kr, 16, stride=128), :]
-                    qs[ph, zc, qq, kr * 16 : kr * 16 + 16, :] = v.astype(BF)
             for r in range(1, NQ):
                 qq, dev = quad_peer(r)
                 remote(
@@ -220,9 +240,8 @@
             return carry
 
         lax.fori_loop(0, NZ, chunk, 0)
-        return total
-
-    def quad_to_z(ph, idle):
+
+    def quad_to_z(ph):
         def chunk(i, carry):
             zc = lax.rem(z + far_first(i), NZ)
             for r in range(1, NQ):
@@ -243,10 +262,11 @@
                     {"space": space_of(q, zc)},
                 ).start()
 
-            idle(i)
             return carry
 
         lax.fori_loop(0, NZ, chunk, 0)
+
+    def z_sum(ph):
         total = zs[ph, z].astype(F32)
         for r in range(1, NZ):
             zz, dev = z_peer(r)
@@ -288,8 +308,9 @@
         lax.fori_loop(0, 7, one, 0)
         gr[ph, z] = mr[ph]
 
-    def z_to_quad(ph, idle):
+    def z_to_quad(ph, early, between):
         def source(j, carry):
+            j = jnp.int32(j)
             zc = lax.rem(z + far_first(7 - j), NZ)
 
             @pl.when(j > 0)
@@ -310,10 +331,12 @@
                     us.at[ph, zc, qq], ur.at[ph, zc, q], u_ss.at[ph, zc, qq], u_rs.at[ph, zc, q], dev
                 ).start()
             ur[ph, zc, q] = us[ph, zc, q]
-            idle(j)
             return carry
 
-        lax.fori_loop(0, NZ, source, 0)
+        source(0, 0)
+        early()
+        lax.fori_loop(1, NZ, source, 0)
+        between()
 
         def take(j, carry):
             zc = lax.rem(z + far_first(7 - j), NZ)
@@ -322,86 +345,95 @@
                 remote(
                     us.at[ph, zc, qq], ur.at[ph, zc, qq], u_ss.at[ph, zc, qq], u_rs.at[ph, zc, qq], dev
                 ).wait_recv()
-            for qq in range(NQ):
-                for k in range(2):
-                    v = ur[ph, zc, qq, k * 32 : k * 32 + 32, :].astype(F32)
-                    big[pl.ds((zc * NQ + qq) * 2 + k, SLAB, stride=64), :] = v
+            res = lax.dot_general(
+                perm[0], ur[ph, zc].reshape(256, 128), NN, preferred_element_type=F32
+            )
+            back[:, pl.ds(pl.multiple_of(zc * 8, 8), 8), :] = res.reshape(SLAB, 8, 128)
             return carry
 
         lax.fori_loop(0, NZ, take, 0)
-
-        def turn(h2, carry):
-            t = big[pl.ds(pl.multiple_of(h2 * 128, 128), 128), :].T
+        for h2 in range(16):
+            t = back[2 * h2 : 2 * h2 + 2].reshape(128, 128).T
             re, im = t[0:64], t[64:128]
-            modes[pl.ds(2 * h2, 64, stride=SLAB), :] = jnp.where(low, re, pltpu.roll(im, 64, 1))
-            modes[pl.ds(2 * h2 + 1, 64, stride=SLAB), :] = jnp.where(low, pltpu.roll(re, 64, 1), im)
-            return carry
-
-        lax.fori_loop(0, 16, turn, 0)
-
-    def nothing(i):
-        pass
+            slab[2 * h2] = jnp.where(low, re, pltpu.roll(im, 64, 1))
+            slab[2 * h2 + 1] = jnp.where(low, pltpu.roll(re, 64, 1), im)
+
+    field_mix = functools.partial(pointwise_tile, 0, field, mix)
+    grad_mix = functools.partial(pointwise_tile, 1, pgr, cot)
 
     quad_send(0)
-    build_kron(True)
-    loads[5].wait()
-    x = quad_to_z(0, functools.partial(pointwise_tile, field))
+    build_kron(0, True)
+    loads[10].wait()
+    quad_to_z(0)
+    some(field_mix, 0, 2)
+    x = z_sum(0)
     dp_out(0, ds, dr, d_ss, d_rs, x)
-    loads[6].wait()
+    loads[11].wait()
     for m in range(8):
         for k in range(2):
             top = sw[m, k].astype(F32)
             bottom = pltpu.roll(top, 64, 1) * sign
             wp[k * 8 + m] = jnp.concatenate([top, bottom], 0).astype(BF)
+    some(field_mix, 2, 5)
     mode_rows = dp_in(0, ds, dr, d_ss, d_rs)
     xkeep[...] = mode_rows
     dp_out(0, ms, mr, m_ss, m_rs, per_mode(mode_rows, NN))
+    some(field_mix, 5, 8)
     mg[...] = jnp.zeros_like(mg)
     dp_in(0, ms, mr, m_ss, m_rs)
     z_send(0)
-    loads[7].wait()
-    z_to_quad(0, nothing)
-
-    loads[8].wait()
-    loads[9].wait()
-    loads[10].wait()
+    loads[12].wait()
+
+    def late_loads():
+        for copy in loads[13:]:
+            copy.wait()
+
+    z_to_quad(0, functools.partial(build_kron, 1, False), late_loads)
+
     c1 = math.sqrt(2.0 / math.pi)
     c3 = c1 * 0.044715
 
-    def section(blk, carry):
-        r0 = pl.multiple_of(blk * 256, 256)
-        pre[...] = lax.dot_general(
-            modes[pl.ds(r0, 256), :].astype(BF), colinv[...], NN, preferred_element_type=F32
-        )
-
-        def tile(t, inner):
+    def pre_part(blk, pre):
+        pre[...] = lax.dot_general(from_slab(blk), colinv[...], NN, preferred_element_type=F32)
+
+    def slopes(blk, pre):
+        for t in range(16):
             ch = blk * 8 + t // 2
-            hh = pl.multiple_of(lax.rem(t, 2) * 16, 16)
-            v = (
-                pre[pl.ds(pl.multiple_of(t * 16, 16), 16), :]
-                + mix[ch, pl.ds(hh, 16), :]
-                + bias[ch]
-            )
+            hh = slice(16 * (t % 2), 16 * (t % 2) + 16)
+            v = pre[16 * t : 16 * t + 16, :] + mix[ch, hh, :] + bias[ch]
             v2 = v * v
-            th = jnp.tanh(v * (c1 + c3 * v2))
-            slope = (0.5 + 0.5 * th) + (v * (0.5 * c1 + 1.5 * c3 * v2)) * (1.0 - th * th)
-            pgr[ch, pl.ds(hh, 16), :] = (cot[ch, pl.ds(hh, 16), :].astype(F32) * slope).astype(BF)
-            return inner
-
-        lax.fori_loop(0, 16, tile, 0)
+            a = 0.5 + 0.5 * jnp.tanh(v * (c1 + c3 * v2))
+            slope = a + a * (1.0 - a) * (v * (2.0 * c1 + 6.0 * c3 * v2))
+            pgr[ch, hh, :] = (cot[ch, hh, :].astype(F32) * slope).astype(BF)
+
+    def grad_part(blk):
         grads = pgr[pl.ds(pl.multiple_of(blk * 8, 8), 8)].reshape(256, W)
-        modes[pl.ds(r0, 256), :] = lax.dot_general(
-            grads, colinvt[...], NN, preferred_element_type=F32
-        )
+        rows = lax.dot_general(grads, colinvt[...], NN, preferred_element_type=F32)
+        to_slab(blk, rows)
+        strip[pl.ds(pl.multiple_of(blk * 8, 8), 8), :] = rows.reshape(8, SLAB, 128).sum(1)
+
+    pre_part(0, pre0)
+
+    def section(i, carry):
+        blk = 2 * i
+        pre_part(blk + 1, pre1)
+        slopes(blk, pre0)
+        grad_part(blk)
+        pre_part(jnp.minimum(blk + 2, 6), pre0)
+        slopes(blk + 1, pre1)
+        grad_part(blk + 1)
         return carry
 
-    lax.fori_loop(0, 8, section, 0)
-
-    total = quad_send(1)
-    strip[...] = total.T
-    build_kron(False)
-    g = quad_to_z(1, mixgrad_tile)
+    lax.fori_loop(0, 4, section, 0)
+
+    quad_send(1)
+    quad_to_z(1)
+    some(mixgrad_tile, 0, 3)
+    g = z_sum(1)
     dp_out(1, ds, dr, d_ss, d_rs, g)
+    some(mixgrad_tile, 3, 8)
+    grad_rows = dp_in(1, ds, dr, d_ss, d_rs)
+    dp_out(1, ms, mr, m_ss, m_rs, per_mode(grad_rows, NT))
 
     spread = (
         lax.broadcasted_iota(jnp.int32, (1024, 64), 0) // 16
@@ -417,15 +449,16 @@
         + lax.dot_general(mid, spread, NN, preferred_element_type=F32)
         + lax.dot_general(lo, spread, NN, preferred_element_type=F32)
     )
-    bias_row = jnp.concatenate([strip[0:1, :] * 32.0, jnp.zeros((63, 64), F32)], 0)
-    pack[...] = jnp.concatenate([part, bias_row], 1).reshape(NZ, 8, 128)
+    bias_row = strip[...].T[0:1, :] * 32.0
+    pack[...] = jnp.concatenate(
+        [part, jnp.concatenate([bias_row, jnp.zeros((63, 64), F32)], 0)], 1
+    ).reshape(NZ, 8, 128)
     for r in range(1, NZ):
         zz, dev = z_peer(r)
         remote(pack.at[zz], prz.at[z], p_ss.at[0, zz], p_rs.at[0, z], dev).start()
     prz[z] = pack[z]
 
-    grad_rows = dp_in(1, ds, dr, d_ss, d_rs)
-    dp_out(1, ms, mr, m_ss, m_rs, per_mode(grad_rows, NT))
+    some(grad_mix, 0, 4)
 
     for r in range(1, NZ):
         zz, dev = z_peer(r)
@@ -436,47 +469,50 @@
         remote(pk.at[0], pdr.at[dp], p_ss.at[1, dd], p_rs.at[1, dp], dev).start()
     pdr[dp] = pk[0]
 
-    x_t = xkeep[...].astype(F32).T
-    for m in range(8):
-        for k in range(2):
-            mine = jnp.where(col_mk == k * 8 + m, x_t, 0.0).astype(BF)
-            prod = lax.dot_general(mine, grad_rows, NN, preferred_element_type=F32)
-            sg[m, k] = prod[0:64] - pltpu.roll(prod[64:128], 64, 1) * sign
-    sg_copy = pltpu.make_async_copy(sg, sg_h, out_sem.at[8])
-    sg_copy.start()
-
     dp_in(1, ms, mr, m_ss, m_rs)
     z_send(1)
 
-    for r in range(1, DP):
-        dd, dev = dp_peer(r)
-        remote(pk.at[0], pdr.at[dd], p_ss.at[1, dd], p_rs.at[1, dd], dev).wait_recv()
-    pk[1] = pdr[...].sum(0)
-    for r in range(1, NQ):
-        qq, dev = quad_peer(r)
-        remote(pk.at[1], pqr.at[q], p_ss.at[2, qq], p_rs.at[2, q], dev).start()
-    pqr[q] = pk[1]
-
-    z_to_quad(1, functools.partial(pointwise_tile, pgr))
-
-    for r in range(1, NQ):
-        qq, dev = quad_peer(r)
-        remote(pk.at[1], pqr.at[qq], p_ss.at[2, qq], p_rs.at[2, qq], dev).wait_recv()
-    pk[2] = pqr[...].sum(0)
-    for r in range(1, NZ):
-        zz, dev = z_peer(r)
-        remote(pk.at[2], pgz.at[z], p_ss.at[3, zz], p_rs.at[3, z], dev).start()
-    pgz[z] = pk[2]
-
-    loads[11].wait()
+    pm_copy = pltpu.make_async_copy(cot, pm_h, out_sem.at[1])
+
+    sg_copy = pltpu.make_async_copy(sg, sg_h, out_sem.at[0])
+
+    def early():
+        some(grad_mix, 4, 7)
+
+        for r in range(1, DP):
+            dd, dev = dp_peer(r)
+            remote(pk.at[0], pdr.at[dd], p_ss.at[1, dd], p_rs.at[1, dd], dev).wait_recv()
+        pk[1] = pdr[...].sum(0)
+        for r in range(1, NQ):
+            qq, dev = quad_peer(r)
+            remote(pk.at[1], pqr.at[q], p_ss.at[2, qq], p_rs.at[2, q], dev).start()
+        pqr[q] = pk[1]
+
+    def totals():
+        x_t = xkeep[...].astype(F32).T
+        for m in range(8):
+            for k in range(2):
+                mine = jnp.where(col_mk == k * 8 + m, x_t, 0.0).astype(BF)
+                prod = lax.dot_general(mine, grad_rows, NN, preferred_element_type=F32)
+                sg[m, k] = prod[0:64] - pltpu.roll(prod[64:128], 64, 1) * sign
+        sg_copy.start()
+        some(grad_mix, 7, 8)
+        pm_copy.start()
+        for r in range(1, NQ):
+            qq, dev = quad_peer(r)
+            remote(pk.at[1], pqr.at[qq], p_ss.at[2, qq], p_rs.at[2, qq], dev).wait_recv()
+        pk[2] = pqr[...].sum(0)
+        for r in range(1, NZ):
+            zz, dev = z_peer(r)
+            remote(pk.at[2], pgz.at[z], p_ss.at[3, zz], p_rs.at[3, z], dev).start()
+        pgz[z] = pk[2]
+
+    z_to_quad(1, early, totals)
+
     for blk in range(8):
-        rows = lax.dot_general(
-            modes[256 * blk : 256 * blk + 256, :].astype(BF), colfwdt[...], NN,
-            preferred_element_type=F32,
-        )
-        chs = slice(8 * blk, 8 * blk + 8)
-        cot[chs] = (rows.reshape(8, SLAB, W) + mix[chs]).astype(BF)
-        pltpu.make_async_copy(cot.at[chs], out_h.at[0, chs], out_sem.at[blk]).start()
+        lrows[256 * blk : 256 * blk + 256, :] = from_slab(blk)
+    l_copy = pltpu.make_async_copy(lrows, l_h, out_sem.at[2])
+    l_copy.start()
 
     for r in range(1, NZ):
         zz, dev = z_peer(r)
@@ -516,47 +552,86 @@
     for r in range(1, NQ):
         qq, dev = quad_peer(r)
         remote(pk.at[1], pqr.at[q], p_ss.at[2, qq], p_rs.at[2, q], dev).wait_send()
-    for blk in range(8):
-        chs = slice(8 * blk, 8 * blk + 8)
-        pltpu.make_async_copy(cot.at[chs], out_h.at[0, chs], out_sem.at[blk]).wait()
     sg_copy.wait()
+    pm_copy.wait()
+    l_copy.wait()
+
+
+def finish(pm_h, l_h, colfwdt_h, sg_h, mg_in, bg_in, out_h, sg_out, mg_out, bg_out,
+           pm, lrows, colfwdt, sg, in_sem, out_sem):
+    loads = [
+        pltpu.make_async_copy(l_h, lrows, in_sem.at[8]),
+        pltpu.make_async_copy(colfwdt_h, colfwdt, in_sem.at[9]),
+        *[
+            pltpu.make_async_copy(pm_h.at[pl.ds(8 * i, 8)], pm.at[pl.ds(8 * i, 8)], in_sem.at[i])
+            for i in range(8)
+        ],
+        pltpu.make_async_copy(sg_h, sg, in_sem.at[10]),
+    ]
+    for copy in loads:
+        copy.start()
+    mg_out[...] = mg_in[...]
+    bg_out[...] = bg_in[...]
+    loads[0].wait()
+    loads[1].wait()
+    stores = []
+    for i in range(8):
+        rows = lax.dot_general(
+            lrows[256 * i : 256 * i + 256, :], colfwdt[...], NN, preferred_element_type=F32
+        )
+        loads[2 + i].wait()
+        chs = slice(8 * i, 8 * i + 8)
+        pm[chs] = (rows.reshape(8, SLAB, W) + pm[chs].astype(F32)).astype(BF)
+        stores.append(pltpu.make_async_copy(pm.at[chs], out_h.at[0, chs], out_sem.at[i]))
+        stores[-1].start()
+    loads[10].wait()
+    stores.append(pltpu.make_async_copy(sg, sg_out, out_sem.at[8]))
+    stores[-1].start()
+    for copy in stores:
+        copy.wait()
 
 
 def per_device(field, cotangent, spectral_weight, mixing_weight, bias):
-    tables = [jnp.asarray(t) for t in build_tables()]
+    colfwd, colinv_t, colinv, colfwd_t, row_fwd, row_inv, perms = [
+        jnp.asarray(t) for t in build_tables()
+    ]
     hbm = pl.BlockSpec(memory_space=pl.ANY)
     vmem = pl.BlockSpec(memory_space=pltpu.VMEM)
     smem = pl.BlockSpec(memory_space=pltpu.SMEM)
     dma = pltpu.SemaphoreType.DMA
-    out = pl.pallas_call(
+    pm, lrows, sg, mg, bg = pl.pallas_call(
         kernel,
         out_shape=(
-            jax.ShapeDtypeStruct((1, C, SLAB, W), BF),
+            jax.ShapeDtypeStruct((C, SLAB, W), BF),
+            jax.ShapeDtypeStruct((C * SLAB, 128), BF),
             jax.ShapeDtypeStruct((8, 2, C, 2 * C), F32),
             jax.ShapeDtypeStruct((C, C), F32),
             jax.ShapeDtypeStruct((1, C), F32),
         ),
         in_specs=[hbm] * 9 + [vmem, smem],
-        out_specs=(hbm, hbm, vmem, vmem),
+        out_specs=(hbm, hbm, hbm, vmem, vmem),
         scratch_shapes=[
             pltpu.VMEM((C, SLAB, W), BF),
             pltpu.VMEM((C, SLAB, W), BF),
             pltpu.VMEM((C, SLAB, W), BF),
             pltpu.VMEM((C, SLAB, W), F32),
-            pltpu.VMEM((1024, 1024), BF),
+            pltpu.VMEM((2, 1024, 1024), BF),
             pltpu.VMEM((8, 2, C, 2 * C), BF),
             pltpu.VMEM((16, 128, 128), BF),
             pltpu.VMEM((W, 128), BF),
             pltpu.VMEM((W, 128), BF),
             pltpu.VMEM((128, W), BF),
-            pltpu.VMEM((128, W), BF),
             pltpu.VMEM((512, 256), BF),
             pltpu.VMEM((512, 128), BF),
-            pltpu.VMEM((C * SLAB, 128), F32),
-            pltpu.VMEM((C * SLAB, 128), F32),
-            pltpu.VMEM((128, C), F32),
+            pltpu.VMEM((3, 256, 256), BF),
+            pltpu.VMEM((SLAB, C, 128), F32),
+            pltpu.VMEM((16, 128, 128), BF),
+            pltpu.VMEM((SLAB, 64, 128), F32),
+            pltpu.VMEM((C * SLAB, 128), BF),
+            pltpu.VMEM((256, W), F32),
             pltpu.VMEM((256, W), F32),
             pltpu.VMEM((128, 128), BF),
+            pltpu.VMEM((C, 128), F32),
             pltpu.VMEM((2, NZ, NQ, 64, 128), BF),
             pltpu.VMEM((2, NZ, NQ, 64, 128), BF),
             pltpu.VMEM((2, NZ, 128, 128), BF),
@@ -576,8 +651,8 @@
             pltpu.VMEM((NQ, 8, 128), F32),
             pltpu.VMEM((NZ, 8, 128), F32),
             pltpu.VMEM((3, 8, 128), F32),
-            dma((12,)),
-            dma((9,)),
+            dma((16,)),
+            dma((3,)),
             dma((2, NZ, NQ)), dma((2, NZ, NQ)),
             dma((2, NZ)), dma((2, NZ)),
             dma((2, DP)), dma((2, DP)),
@@ -592,8 +667,31 @@
         cost_estimate=pl.CostEstimate(
             flops=20_000_000_000, bytes_accessed=16_000_000, transcendentals=2_000_000
         ),
-    )(field, cotangent, spectral_weight, *tables, mixing_weight, bias)
-    field_grad, spectral_grad, mixing_grad, bias_grad = out
+    )(field, cotangent, spectral_weight, colfwd, colinv_t, colinv, row_fwd, row_inv, perms,
+      mixing_weight, bias)
+    field_grad, spectral_grad, mixing_grad, bias_grad = pl.pallas_call(
+        finish,
+        out_shape=(
+            jax.ShapeDtypeStruct((1, C, SLAB, W), BF),
+            jax.ShapeDtypeStruct((8, 2, C, 2 * C), F32),
+            jax.ShapeDtypeStruct((C, C), F32),
+            jax.ShapeDtypeStruct((1, C), F32),
+        ),
+        in_specs=[hbm] * 4 + [vmem, vmem],
+        out_specs=(hbm, hbm, vmem, vmem),
+        scratch_shapes=[
+            pltpu.VMEM((C, SLAB, W), BF),
+            pltpu.VMEM((C * SLAB, 128), BF),
+            pltpu.VMEM((128, W), BF),
+            pltpu.VMEM((8, 2, C, 2 * C), F32),
+            dma((11,)),
+            dma((9,)),
+        ],
+        compiler_params=pltpu.CompilerParams(vmem_limit_bytes=58 * 1024 * 1024),
+        cost_estimate=pl.CostEstimate(
+            flops=600_000_000, bytes_accessed=10_000_000, transcendentals=0
+        ),
+    )(pm, lrows, colfwd_t, sg, mg, bg)
     return field_grad, spectral_grad, mixing_grad, bias_grad.reshape(C)
 
 

time: 123 us -> 110 us (0.89)
  Pallas kernels: 116 us -> 109 us
  local copies, waits for them, and re-layouts: 7 us -> 0 us
    unnamed x10 -> x0, local copies, waits for them, and re-layouts: 7 us -> none
    pallas_call x1 -> x2, Pallas kernels: 116 us -> 109 us  [the longest x1 102 us: per_device(): pl.pallas_call(kernel, out_shape=(jax.ShapeDtypeStruct((C, SLAB, W), BF),...]
where the time goes in v1:
time: 110 us; the launch traced here: 109 us
  Pallas kernels  109 us (99%)
    pallas_call x1, Pallas kernels, per_device(): pl.pallas_call(kernel, out_shape=(jax.ShapeDtypeStruct((C, SLAB, W), BF),...  102 us
    pallas_call x1, Pallas kernels, per_device(): pl.pallas_call(finish, out_shape=(jax.ShapeDtypeStruct((1, C, SLAB, W), B...  7.09 us

profile of v1, /device:TPU:1, one launch (start us, length us, event | category | flops | bytes accessed | tf_op | source)
XLA Modules:
  0.0 109.5 jit_solution(11802912868771542086)
XLA Ops:
  0.6 101.6 %shard_map.147 = (bf16[64,32,1024]{2,1,0:T(8,128)(2,1)}, bf16[2048,128]{1,0:T(8,128)(2,1)}, f32[8,2,64,128]{3,2,1,0:T(8,128)}, f32[64,64]{1,0:T(8,128)}, f32[1,64]{1,0:T(1,128)}) custom-call(bf16[1,64,32,1024]{3,2,1,0:T(8,128)(2,1)} %field_h.1, bf16[1,64,32,1024]{3,2,1,0:T(8,128)(2,1)} %cot_h.1, bf16[8,2,64,128]{3,2,1,0:T(8,128)(2,1)} %sw_h.1, ...), custom_call_target="tpu_custom_call" | custom-call | flops 20000000000 | bytes 16000000 | tf_op jit(solution)/shard_map/pallas_call | solution.py:602
  102.2 7.1 %shard_map.148 = (bf16[1,64,32,1024]{3,2,1,0:T(8,128)(2,1)}, f32[8,2,64,128]{3,2,1,0:T(8,128)}, f32[64,64]{1,0:T(8,128)}, f32[1,64]{1,0:T(1,128)}) custom-call(bf16[64,32,1024]{2,1,0:T(8,128)(2,1)} %get-tuple-element.13.pm_h, bf16[2048,128]{1,0:T(8,128)(2,1)} %get-tuple-element.14.l_h, bf16[128,1024]{1,0:T(8,128)(2,1)} %constant.17.clone.colfwdt_h, ...), custom_call_target="tpu_custom_call" | custom-call | flops 600000000 | bytes 10000000 | tf_op jit(solution)/shard_map/pallas_call | solution.py:672

commit v2 on v1

--- a/solution.py
+++ b/solution.py
@@ -93,11 +93,10 @@
     mw, bias,
     pm_h, l_h, sg_h, mg_out, bg_out,
     field, cot, pgr, mix, kron, sw, wp, colfwd, colinvt, colinv, rowf, rowi,
-    perm, slab, big, back, lrows, pre0, pre1, xkeep, strip,
+    perm, slab, big, back, lrows, pre0, pre1, xkeep, strip, bcol,
     qs, qr, zs, zr, ds, dr, ms, mr, gr, us, ur, sg, mg, pack, prz, pdr, pqr, pgz, pk,
     in_sem, out_sem,
-    q_ss, q_rs, z_ss, z_rs, d_ss, d_rs, m_ss, m_rs, g_ss, g_rs, u_ss, u_rs,
-    p_ss, p_rs,
+    s_ss, q_rs, z_rs, d_rs, m_rs, g_rs, u_rs, p_ss, p_rs,
 ):
     dp = lax.axis_index("dp")
     sp = lax.axis_index("space")
@@ -124,6 +123,12 @@
             src_ref=src, dst_ref=dst, send_sem=ss, recv_sem=rs,
             device_id=dev, device_id_type=pl.DeviceIdType.MESH,
         )
+
+    def arrived(ref, sem):
+        remote(ref, ref, sem, sem, quad_peer(1)[1]).wait_recv()
+
+    def left(ref, sem):
+        remote(ref, ref, sem, sem, quad_peer(1)[1]).wait_send()
 
     loads = [
         pltpu.make_async_copy(colfwd_h, colfwd, in_sem.at[0]),
@@ -168,6 +173,12 @@
         rows = slab[:, pl.ds(start, 8), :].reshape(256, 128).astype(BF)
         return lax.dot_general(perm[1], rows, NN, preferred_element_type=F32).astype(BF)
 
+    def bias_rows(ch, carry):
+        bcol[ch] = jnp.full((16, 128), bias[ch], F32)
+        return carry
+
+    lax.fori_loop(0, C, bias_rows, 0)
+
     loads[0].wait()
     loads[9].wait()
     for i in range(8):
@@ -195,12 +206,15 @@
             )
             kron[n, 256 * i : 256 * i + 256, :] = jnp.where(same, full, 0.0).astype(BF)
 
-    def pointwise_tile(n, source, target, i):
+    def pointwise_tile(n, source, target, offset, i):
         hb = pl.multiple_of((i // 4) * 16, 16)
         wq = pl.multiple_of(lax.rem(i, 4) * 256, 256)
         rhs = source[:, pl.ds(hb, 16), pl.ds(wq, 256)].reshape(1024, 256)
         res = lax.dot_general(kron[n], rhs, NN, preferred_element_type=F32)
-        target[:, pl.ds(hb, 16), pl.ds(wq, 256)] = res.reshape(64, 16, 256).astype(target.dtype)
+        res = res.reshape(64, 16, 256)
+        if offset is not None:
+            res = res + jnp.concatenate([offset[...], offset[...]], -1)
+        target[:, pl.ds(hb, 16), pl.ds(wq, 256)] = res.astype(target.dtype)
 
     def some(tile, first, last):
         def one(i, carry):
@@ -234,7 +248,7 @@
             for r in range(1, NQ):
                 qq, dev = quad_peer(r)
                 remote(
-                    qs.at[ph, zc, qq], qr.at[ph, zc, q], q_ss.at[ph, zc, qq], q_rs.at[ph, zc, q], dev
+                    qs.at[ph, zc, qq], qr.at[ph, zc, q], s_ss.at[0], q_rs.at[ph, zc], dev
                 ).start()
             qr[ph, zc, q] = qs[ph, zc, q]
             return carry
@@ -244,11 +258,7 @@
     def quad_to_z(ph):
         def chunk(i, carry):
             zc = lax.rem(z + far_first(i), NZ)
-            for r in range(1, NQ):
-                qq, dev = quad_peer(r)
-                remote(
-                    qs.at[ph, zc, qq], qr.at[ph, zc, qq], q_ss.at[ph, zc, qq], q_rs.at[ph, zc, qq], dev
-                ).wait_recv()
+            arrived(qr.at[ph, zc, pl.ds(0, 3)], q_rs.at[ph, zc])
             x = qr[ph, zc].reshape(256, 128)
             b = lax.dot_general(rowf[...], x, NN, preferred_element_type=F32)
             straight = jnp.where(low128, b[0:128], b[384:512])
@@ -258,7 +268,7 @@
             @pl.when(i < 7)
             def _():
                 remote(
-                    zs.at[ph, zc], zr.at[ph, z], z_ss.at[ph, zc], z_rs.at[ph, z],
+                    zs.at[ph, zc], zr.at[ph, z], s_ss.at[1], z_rs.at[ph],
                     {"space": space_of(q, zc)},
                 ).start()
 
@@ -268,9 +278,9 @@
 
     def z_sum(ph):
         total = zs[ph, z].astype(F32)
+        arrived(zr.at[ph, pl.ds(0, 7)], z_rs.at[ph])
         for r in range(1, NZ):
             zz, dev = z_peer(r)
-            remote(zs.at[ph, zz], zr.at[ph, zz], z_ss.at[ph, zz], z_rs.at[ph, zz], dev).wait_recv()
             total = total + zr[ph, zz].astype(F32)
         return total.astype(BF)
 
@@ -278,13 +288,11 @@
         src[ph] = value.reshape(DP, 16, 128)
         for r in range(1, DP):
             dd, dev = dp_peer(r)
-            remote(src.at[ph, dd], dst.at[ph, dp], ss.at[ph, dd], rs.at[ph, dp], dev).start()
+            remote(src.at[ph, dd], dst.at[ph, dp], ss, rs.at[ph], dev).start()
         dst[ph, dp] = src[ph, dp]
 
-    def dp_in(ph, src, dst, ss, rs):
-        for r in range(1, DP):
-            dd, dev = dp_peer(r)
-            remote(src.at[ph, dd], dst.at[ph, dd], ss.at[ph, dd], rs.at[ph, dd], dev).wait_recv()
+    def dp_in(ph, dst, rs):
+        arrived(dst.at[ph, pl.ds(0, 7)], rs.at[ph])
         return dst[ph].reshape(128, 128)
 
     row_mk = lax.rem(lax.broadcasted_iota(jnp.int32, (128, 128), 0), 16)
@@ -301,7 +309,7 @@
         def one(i, carry):
             zz = lax.rem(z + far_first(i), NZ)
             remote(
-                mr.at[ph], gr.at[ph, z], g_ss.at[ph, zz], g_rs.at[ph, z], {"space": space_of(q, zz)}
+                mr.at[ph], gr.at[ph, z], s_ss.at[4], g_rs.at[ph, z], {"space": space_of(q, zz)}
             ).start()
             return carry
 
@@ -315,10 +323,7 @@
 
             @pl.when(j > 0)
             def _():
-                remote(
-                    mr.at[ph], gr.at[ph, zc], g_ss.at[ph, zc], g_rs.at[ph, zc],
-                    {"space": space_of(q, lax.rem(z + jnp.maximum(far_first(7 - j), 1), NZ))},
-                ).wait_recv()
+                arrived(gr.at[ph, zc], g_rs.at[ph, zc])
 
             t = lax.dot_general(
                 rowi[...], gr[ph, zc].reshape(128, 128), NN, preferred_element_type=F32
@@ -328,7 +333,7 @@
             for r in range(1, NQ):
                 qq, dev = quad_peer(r)
                 remote(
-                    us.at[ph, zc, qq], ur.at[ph, zc, q], u_ss.at[ph, zc, qq], u_rs.at[ph, zc, q], dev
+                    us.at[ph, zc, qq], ur.at[ph, zc, q], s_ss.at[5], u_rs.at[ph, zc], dev
                 ).start()
             ur[ph, zc, q] = us[ph, zc, q]
             return carry
@@ -340,11 +345,7 @@
 
         def take(j, carry):
             zc = lax.rem(z + far_first(7 - j), NZ)
-            for r in range(1, NQ):
-                qq, dev = quad_peer(r)
-                remote(
-                    us.at[ph, zc, qq], ur.at[ph, zc, qq], u_ss.at[ph, zc, qq], u_rs.at[ph, zc, qq], dev
-                ).wait_recv()
+            arrived(ur.at[ph, zc, pl.ds(0, 3)], u_rs.at[ph, zc])
             res = lax.dot_general(
                 perm[0], ur[ph, zc].reshape(256, 128), NN, preferred_element_type=F32
             )
@@ -358,8 +359,8 @@
             slab[2 * h2] = jnp.where(low, re, pltpu.roll(im, 64, 1))
             slab[2 * h2 + 1] = jnp.where(low, pltpu.roll(re, 64, 1), im)
 
-    field_mix = functools.partial(pointwise_tile, 0, field, mix)
-    grad_mix = functools.partial(pointwise_tile, 1, pgr, cot)
+    field_mix = functools.partial(pointwise_tile, 0, field, mix, bcol)
+    grad_mix = functools.partial(pointwise_tile, 1, pgr, cot, None)
 
     quad_send(0)
     build_kron(0, True)
@@ -367,7 +368,7 @@
     quad_to_z(0)
     some(field_mix, 0, 2)
     x = z_sum(0)
-    dp_out(0, ds, dr, d_ss, d_rs, x)
+    dp_out(0, ds, dr, s_ss.at[2], d_rs, x)
     loads[11].wait()
     for m in range(8):
         for k in range(2):
@@ -375,12 +376,12 @@
             bottom = pltpu.roll(top, 64, 1) * sign
             wp[k * 8 + m] = jnp.concatenate([top, bottom], 0).astype(BF)
     some(field_mix, 2, 5)
-    mode_rows = dp_in(0, ds, dr, d_ss, d_rs)
+    mode_rows = dp_in(0, dr, d_rs)
     xkeep[...] = mode_rows
-    dp_out(0, ms, mr, m_ss, m_rs, per_mode(mode_rows, NN))
+    dp_out(0, ms, mr, s_ss.at[3], m_rs, per_mode(mode_rows, NN))
     some(field_mix, 5, 8)
     mg[...] = jnp.zeros_like(mg)
-    dp_in(0, ms, mr, m_ss, m_rs)
+    dp_in(0, mr, m_rs)
     z_send(0)
     loads[12].wait()
 
@@ -400,11 +401,13 @@
         for t in range(16):
             ch = blk * 8 + t // 2
             hh = slice(16 * (t % 2), 16 * (t % 2) + 16)
-            v = pre[16 * t : 16 * t + 16, :] + mix[ch, hh, :] + bias[ch]
-            v2 = v * v
-            a = 0.5 + 0.5 * jnp.tanh(v * (c1 + c3 * v2))
-            slope = a + a * (1.0 - a) * (v * (2.0 * c1 + 6.0 * c3 * v2))
-            pgr[ch, hh, :] = (cot[ch, hh, :].astype(F32) * slope).astype(BF)
+            v = pre[16 * t : 16 * t + 16, :] + mix[ch, hh, :]
+            th = jnp.tanh((v * (c1 + c3 * (v * v))).astype(BF))
+            vb = v.astype(BF)
+            a = th * BF(0.5) + BF(0.5)
+            rise = vb * (vb * vb * BF(6.0 * c3) + BF(2.0 * c1))
+            slope = a + a * (BF(1.0) - a) * rise
+            pgr[ch, hh, :] = cot[ch, hh, :] * slope
 
     def grad_part(blk):
         grads = pgr[pl.ds(pl.multiple_of(blk * 8, 8), 8)].reshape(256, W)
@@ -430,10 +433,10 @@
     quad_to_z(1)
     some(mixgrad_tile, 0, 3)
     g = z_sum(1)
-    dp_out(1, ds, dr, d_ss, d_rs, g)
+    dp_out(1, ds, dr, s_ss.at[2], d_rs, g)
     some(mixgrad_tile, 3, 8)
-    grad_rows = dp_in(1, ds, dr, d_ss, d_rs)
-    dp_out(1, ms, mr, m_ss, m_rs, per_mode(grad_rows, NT))
+    grad_rows = dp_in(1, dr, d_rs)
+    dp_out(1, ms, mr, s_ss.at[3], m_rs, per_mode(grad_rows, NT))
 
     spread = (
         lax.broadcasted_iota(jnp.int32, (1024, 64), 0) // 16
@@ -455,21 +458,19 @@
     ).reshape(NZ, 8, 128)
     for r in range(1, NZ):
         zz, dev = z_peer(r)
-        remote(pack.at[zz], prz.at[z], p_ss.at[0, zz], p_rs.at[0, z], dev).start()
+        remote(pack.at[zz], prz.at[z], p_ss.at[0], p_rs.at[0], dev).start()
     prz[z] = pack[z]
 
     some(grad_mix, 0, 4)
 
-    for r in range(1, NZ):
-        zz, dev = z_peer(r)
-        remote(pack.at[zz], prz.at[zz], p_ss.at[0, zz], p_rs.at[0, zz], dev).wait_recv()
+    arrived(prz.at[pl.ds(0, 7)], p_rs.at[0])
     pk[0] = prz[...].sum(0)
     for r in range(1, DP):
         dd, dev = dp_peer(r)
-        remote(pk.at[0], pdr.at[dp], p_ss.at[1, dd], p_rs.at[1, dp], dev).start()
+        remote(pk.at[0], pdr.at[dp], p_ss.at[1], p_rs.at[1], dev).start()
     pdr[dp] = pk[0]
 
-    dp_in(1, ms, mr, m_ss, m_rs)
+    dp_in(1, mr, m_rs)
     z_send(1)
 
     pm_copy = pltpu.make_async_copy(cot, pm_h, out_sem.at[1])
@@ -479,13 +480,11 @@
     def early():
         some(grad_mix, 4, 7)
 
-        for r in range(1, DP):
-            dd, dev = dp_peer(r)
-            remote(pk.at[0], pdr.at[dd], p_ss.at[1, dd], p_rs.at[1, dd], dev).wait_recv()
+        arrived(pdr.at[pl.ds(0, 7)], p_rs.at[1])
         pk[1] = pdr[...].sum(0)
         for r in range(1, NQ):
             qq, dev = quad_peer(r)
-            remote(pk.at[1], pqr.at[q], p_ss.at[2, qq], p_rs.at[2, q], dev).start()
+            remote(pk.at[1], pqr.at[q], p_ss.at[2], p_rs.at[2], dev).start()
         pqr[q] = pk[1]
 
     def totals():
@@ -498,13 +497,11 @@
         sg_copy.start()
         some(grad_mix, 7, 8)
         pm_copy.start()
-        for r in range(1, NQ):
-            qq, dev = quad_peer(r)
-            remote(pk.at[1], pqr.at[qq], p_ss.at[2, qq], p_rs.at[2, qq], dev).wait_recv()
+        arrived(pqr.at[pl.ds(0, 3)], p_rs.at[2])
         pk[2] = pqr[...].sum(0)
         for r in range(1, NZ):
             zz, dev = z_peer(r)
-            remote(pk.at[2], pgz.at[z], p_ss.at[3, zz], p_rs.at[3, z], dev).start()
+            remote(pk.at[2], pgz.at[z], p_ss.at[3], p_rs.at[3], dev).start()
         pgz[z] = pk[2]
 
     z_to_quad(1, early, totals)
@@ -514,44 +511,22 @@
     l_copy = pltpu.make_async_copy(lrows, l_h, out_sem.at[2])
     l_copy.start()
 
-    for r in range(1, NZ):
-        zz, dev = z_peer(r)
-        remote(pk.at[2], pgz.at[zz], p_ss.at[3, zz], p_rs.at[3, zz], dev).wait_recv()
+    arrived(pgz.at[pl.ds(0, 7)], p_rs.at[3])
     norm = 1.0 / math.sqrt(DP * H * W)
     whole = pgz[...].reshape(64, 128) * norm
     mg_out[...] = whole[:, 0:64]
     bg_out[...] = whole[0:1, 64:128]
 
-    for ph in range(2):
-
-        def drain(i, carry):
-            for r in range(1, NQ):
-                qq, dev = quad_peer(r)
-                remote(
-                    qs.at[ph, i, qq], qr.at[ph, i, q], q_ss.at[ph, i, qq], q_rs.at[ph, i, q], dev
-                ).wait_send()
-                remote(
-                    us.at[ph, i, qq], ur.at[ph, i, q], u_ss.at[ph, i, qq], u_rs.at[ph, i, q], dev
-                ).wait_send()
-            return carry
-
-        lax.fori_loop(0, NZ, drain, 0)
-        for r in range(1, NZ):
-            zz, dev = z_peer(r)
-            remote(zs.at[ph, zz], zr.at[ph, z], z_ss.at[ph, zz], z_rs.at[ph, z], dev).wait_send()
-            remote(mr.at[ph], gr.at[ph, z], g_ss.at[ph, zz], g_rs.at[ph, z], dev).wait_send()
-            dd, dev = dp_peer(r)
-            remote(ds.at[ph, dd], dr.at[ph, dp], d_ss.at[ph, dd], d_rs.at[ph, dp], dev).wait_send()
-            remote(ms.at[ph, dd], mr.at[ph, dp], m_ss.at[ph, dd], m_rs.at[ph, dp], dev).wait_send()
-    for r in range(1, NZ):
-        zz, dev = z_peer(r)
-        remote(pack.at[zz], prz.at[z], p_ss.at[0, zz], p_rs.at[0, z], dev).wait_send()
-        remote(pk.at[2], pgz.at[z], p_ss.at[3, zz], p_rs.at[3, z], dev).wait_send()
-        dd, dev = dp_peer(r)
-        remote(pk.at[0], pdr.at[dp], p_ss.at[1, dd], p_rs.at[1, dp], dev).wait_send()
-    for r in range(1, NQ):
-        qq, dev = quad_peer(r)
-        remote(pk.at[1], pqr.at[q], p_ss.at[2, qq], p_rs.at[2, q], dev).wait_send()
+    left(qs.at[:, :, pl.ds(0, 3)], s_ss.at[0])
+    left(zs.at[:, pl.ds(0, 7)], s_ss.at[1])
+    left(ds.at[:, pl.ds(0, 7)], s_ss.at[2])
+    left(ms.at[:, pl.ds(0, 7)], s_ss.at[3])
+    left(gr.at[:, pl.ds(0, 7)], s_ss.at[4])
+    left(us.at[:, :, pl.ds(0, 3)], s_ss.at[5])
+    left(prz.at[pl.ds(0, 7)], p_ss.at[0])
+    left(pdr.at[pl.ds(0, 7)], p_ss.at[1])
+    left(pqr.at[pl.ds(0, 3)], p_ss.at[2])
+    left(pgz.at[pl.ds(0, 7)], p_ss.at[3])
     sg_copy.wait()
     pm_copy.wait()
     l_copy.wait()
@@ -632,6 +607,7 @@
             pltpu.VMEM((256, W), F32),
             pltpu.VMEM((128, 128), BF),
             pltpu.VMEM((C, 128), F32),
+            pltpu.VMEM((C, 16, 128), F32),
             pltpu.VMEM((2, NZ, NQ, 64, 128), BF),
             pltpu.VMEM((2, NZ, NQ, 64, 128), BF),
             pltpu.VMEM((2, NZ, 128, 128), BF),
@@ -653,13 +629,9 @@
             pltpu.VMEM((3, 8, 128), F32),
             dma((16,)),
             dma((3,)),
-            dma((2, NZ, NQ)), dma((2, NZ, NQ)),
-            dma((2, NZ)), dma((2, NZ)),
-            dma((2, DP)), dma((2, DP)),
-            dma((2, DP)), dma((2, DP)),
-            dma((2, NZ)), dma((2, NZ)),
-            dma((2, NZ, NQ)), dma((2, NZ, NQ)),
-            dma((4, 8)), dma((4, 8)),
+            dma((6,)),
+            dma((2, NZ)), dma((2,)), dma((2,)), dma((2,)), dma((2, NZ)), dma((2, NZ)),
+            dma((4,)), dma((4,)),
         ],
         compiler_params=pltpu.CompilerParams(
             collective_id=0, has_side_effects=True, vmem_limit_bytes=58 * 1024 * 1024

time: 110 us -> 104 us (0.945)
  Pallas kernels: 109 us -> 103 us
    pallas_call x1, Pallas kernels: 102 us -> 96 us  [per_device(): pl.pallas_call(kernel, out_shape=(jax.ShapeDtypeStruct((C, SLAB, W), BF),...]
where the time goes in v2:
time: 104 us
  Pallas kernels  103 us (99%)
    pallas_call x1, Pallas kernels, per_device(): pl.pallas_call(kernel, out_shape=(jax.ShapeDtypeStruct((C, SLAB, W), BF),...  96 us
    pallas_call x1, Pallas kernels, per_device(): pl.pallas_call(finish, out_shape=(jax.ShapeDtypeStruct((1, C, SLAB, W), B...  7.08 us

profile of v2, /device:TPU:1, one launch (start us, length us, event | category | flops | bytes accessed | tf_op | source)
XLA Modules:
  0.0 103.9 jit_solution(15003834695901661369)
XLA Ops:
  0.6 96.0 %shard_map.147 = (bf16[64,32,1024]{2,1,0:T(8,128)(2,1)}, bf16[2048,128]{1,0:T(8,128)(2,1)}, f32[8,2,64,128]{3,2,1,0:T(8,128)}, f32[64,64]{1,0:T(8,128)}, f32[1,64]{1,0:T(1,128)}) custom-call(bf16[1,64,32,1024]{3,2,1,0:T(8,128)(2,1)} %field_h.1, bf16[1,64,32,1024]{3,2,1,0:T(8,128)(2,1)} %cot_h.1, bf16[8,2,64,128]{3,2,1,0:T(8,128)(2,1)} %sw_h.1, ...), custom_call_target="tpu_custom_call" | custom-call | flops 20000000000 | bytes 16000000 | tf_op jit(solution)/shard_map/pallas_call | solution.py:577
  96.7 7.1 %shard_map.148 = (bf16[1,64,32,1024]{3,2,1,0:T(8,128)(2,1)}, f32[8,2,64,128]{3,2,1,0:T(8,128)}, f32[64,64]{1,0:T(8,128)}, f32[1,64]{1,0:T(1,128)}) custom-call(bf16[64,32,1024]{2,1,0:T(8,128)(2,1)} %get-tuple-element.13.pm_h, bf16[2048,128]{1,0:T(8,128)(2,1)} %get-tuple-element.14.l_h, bf16[128,1024]{1,0:T(8,128)(2,1)} %constant.17.clone.colfwdt_h, ...), custom_call_target="tpu_custom_call" | custom-call | flops 600000000 | bytes 10000000 | tf_op jit(solution)/shard_map/pallas_call | solution.py:644

commit v3 on v2

--- a/solution.py
+++ b/solution.py
@@ -402,10 +402,10 @@
             ch = blk * 8 + t // 2
             hh = slice(16 * (t % 2), 16 * (t % 2) + 16)
             v = pre[16 * t : 16 * t + 16, :] + mix[ch, hh, :]
-            th = jnp.tanh((v * (c1 + c3 * (v * v))).astype(BF))
             vb = v.astype(BF)
-            a = th * BF(0.5) + BF(0.5)
-            rise = vb * (vb * vb * BF(6.0 * c3) + BF(2.0 * c1))
+            v2 = vb * vb
+            a = jnp.tanh(vb * (v2 * BF(c3) + BF(c1))) * BF(0.5) + BF(0.5)
+            rise = vb * (v2 * BF(6.0 * c3) + BF(2.0 * c1))
             slope = a + a * (BF(1.0) - a) * rise
             pgr[ch, hh, :] = cot[ch, hh, :] * slope
 

time: 104 us -> 103 us (level)
  no operation moved by 1% of the time
where the time goes in v3:
time: 103 us
  Pallas kernels  102 us (99%)
    pallas_call x1, Pallas kernels, per_device(): pl.pallas_call(kernel, out_shape=(jax.ShapeDtypeStruct((C, SLAB, W), BF),...  95.3 us
    pallas_call x1, Pallas kernels, per_device(): pl.pallas_call(finish, out_shape=(jax.ShapeDtypeStruct((1, C, SLAB, W), B...  7.08 us

profile of v3, /device:TPU:1, one launch (start us, length us, event | category | flops | bytes accessed | tf_op | source)
XLA Modules:
  0.0 103.2 jit_solution(4194704973965774021)
XLA Ops:
  0.6 95.3 %shard_map.147 = (bf16[64,32,1024]{2,1,0:T(8,128)(2,1)}, bf16[2048,128]{1,0:T(8,128)(2,1)}, f32[8,2,64,128]{3,2,1,0:T(8,128)}, f32[64,64]{1,0:T(8,128)}, f32[1,64]{1,0:T(1,128)}) custom-call(bf16[1,64,32,1024]{3,2,1,0:T(8,128)(2,1)} %field_h.1, bf16[1,64,32,1024]{3,2,1,0:T(8,128)(2,1)} %cot_h.1, bf16[8,2,64,128]{3,2,1,0:T(8,128)(2,1)} %sw_h.1, ...), custom_call_target="tpu_custom_call" | custom-call | flops 20000000000 | bytes 16000000 | tf_op jit(solution)/shard_map/pallas_call | solution.py:577
  95.9 7.1 %shard_map.148 = (bf16[1,64,32,1024]{3,2,1,0:T(8,128)(2,1)}, f32[8,2,64,128]{3,2,1,0:T(8,128)}, f32[64,64]{1,0:T(8,128)}, f32[1,64]{1,0:T(1,128)}) custom-call(bf16[64,32,1024]{2,1,0:T(8,128)(2,1)} %get-tuple-element.13.pm_h, bf16[2048,128]{1,0:T(8,128)(2,1)} %get-tuple-element.14.l_h, bf16[128,1024]{1,0:T(8,128)(2,1)} %constant.17.clone.colfwdt_h, ...), custom_call_target="tpu_custom_call" | custom-call | flops 600000000 | bytes 10000000 | tf_op jit(solution)/shard_map/pallas_call | solution.py:644
